TPU v7x, 32 devices: a whole 2x2x4 slice. The times are simulated.
32 devices in a mesh: dp: 8 (over z, x), sp: 4 (over y, core).
Axes of the slice: x: 2, y: 2, z: 4, core: 2. Of those that a mesh axis runs over, the one named last changes fastest.
Arguments:
- tokens: bfloat16 [512, 32, 768], P('sp', 'dp'), may hold values from -6 to 6
- lengths: int32 [32], P('dp'), may hold values from 1 to 512, as said below
- w_query: bfloat16 [768, 768], replicated, may hold values from -0.21875 to 0.21875
- b_query: bfloat16 [768], replicated, may hold values from -2 to 2
- w_key: bfloat16 [768, 768], replicated, may hold values from -0.21875 to 0.21875
- w_value: bfloat16 [768, 768], replicated, may hold values from -0.21875 to 0.21875
- b_value: bfloat16 [768], replicated, may hold values from -2 to 2
- w_out: bfloat16 [768, 768], replicated, may hold values from -1.75 to 1.75
- b_out: bfloat16 [768], replicated, may hold values from -2 to 2
- gain_attn: bfloat16 [768], replicated, may hold values from 0.5 to 1.5
- shift_attn: bfloat16 [768], replicated, may hold values from -2 to 2
- w_up: bfloat16 [768, 3072], replicated, may hold values from -0.21875 to 0.21875
- b_up: bfloat16 [3072], replicated, may hold values from -3 to 3
- w_down: bfloat16 [3072, 768], replicated, may hold values from -0.109375 to 0.109375
- b_down: bfloat16 [768], replicated, may hold values from -2 to 2
- gain_ffn: bfloat16 [768], replicated, may hold values from 0.5 to 1.5
- shift_ffn: bfloat16 [768], replicated, may hold values from -2 to 2
- cotangent: bfloat16 [512, 32, 768], P('sp', 'dp'), may hold values from -6 to 6
Outputs:
- mixed: bfloat16 [512, 32, 768], P('sp', 'dp')
- grad_tokens: bfloat16 [512, 32, 768], P('sp', 'dp')
- grad_w_query: float32 [768, 768], P('dp')
- grad_b_query: float32 [768], P('dp')
- grad_w_key: float32 [768, 768], P('dp')
- grad_w_value: float32 [768, 768], P('dp')
- grad_b_value: float32 [768], P('dp')
- grad_w_out: float32 [768, 768], P('dp')
- grad_b_out: float32 [768], P('dp')
- grad_gain_attn: float32 [768], P('dp')
- grad_shift_attn: float32 [768], P('dp')
- grad_w_up: float32 [768, 3072], P('dp')
- grad_b_up: float32 [3072], P('dp')
- grad_w_down: float32 [3072, 768], P('dp')
- grad_b_down: float32 [768], P('dp')
- grad_gain_ffn: float32 [768], P('dp')
- grad_shift_ffn: float32 [768], P('dp')
Inputs may be any that keep to these rules, and one draw needn't show every extreme that they name: Each pair's first lengths slots are live keys; in every aligned block of 4 pairs (those of one index of dp) at least one pair has all 512 slots live.
All inputs are finite; a program needn't handle non-finite values.
Results may differ from a plain program's by a relative error of at most 0.018.
Values may be sent and summed in bfloat16 or wider, within the bound.
A program may use at most 192 MiB of HBM per device.

v0:
```python
import functools

import jax
import jax.numpy as jnp
from jax import lax
from jax.experimental import pallas as pl
from jax.experimental.pallas import tpu as pltpu
from jax.sharding import PartitionSpec as P

HEADS = 12
HD = 64
EPS = 1e-05
MESH_ID = pl.DeviceIdType.MESH
BF = jnp.bfloat16
F32 = jnp.float32


def nn(left, right):
    return jnp.dot(left, right, preferred_element_type=F32)


def nt(left, right):
    return lax.dot_general(left, right, (((1,), (1,)), ((), ())), preferred_element_type=F32)


def tn(left, right):
    return lax.dot_general(left, right, (((0,), (0,)), ((), ())), preferred_element_type=F32)


def aligned(start, step=128):
    return pl.multiple_of(start, step)


UNITS = (
    ("d", 0, 0, 256), ("d", 0, 256, 256), ("d", 0, 512, 256), ("d", 1, 0, 384), ("d", 1, 384, 384), ("d", 2, 0, 384),
    ("d", 2, 384, 384), ("u", 0, 0, 1024), ("u", 1, 0, 1024), ("u", 2, 0, 1024), ("o",), ("p", 0, 3, 0),
    ("p", 0, 1, 1), ("p", 1, 2, 1), ("p", 0, 1, 2), ("p", 1, 1, 2), ("p", 2, 1, 2),
)
PATH = (
    "c102y", "c120Y", "c0y12", "c102y", "c0y12", "cy120", "c01y2", "cy120", "cy012", "c0y12", "c120Y", "c012y",
    "c012y", "c0y12", "c012Y", "c0y12", "c0y12",
)
ORDER = (
    "M", 0, 1, 2, 3, 0, 1, 2, 4, 5, 6, "X", "I0", 3, 4, "I1", 5, 6, 0, 2, "H0", 1, 7, 4, 8, 5, 3, 7, 2, 9, "F", 6, 1,
    8, 4, 0, "A", 9, 5, 2, 10, 3, 1, "B0", 6, 4, 10, 0, 11, 5, 2, "B2", 7, 3, 11, 4, 12, 9, 5, 13, "B4", 12, 13, 10,
    8, "T", "K", 1, 6, 0, 2, 7, 3, 11, 4, 14, 15, 16, "V0", 12, 14, 15, 16, "V1", 9, 5, 10, 13, 6, 11, 12, 8, 7, 9,
    14, 0, 11, 3, 15, 12, 8, 13, 6, 16, 9, "V2", 11, 14, 15, 12, 10, 13, 16, 7, 8, "V3", 9, 14, 15, 11, 12, 16, 13,
    10, 7, "V4", 15, 8, 16, 14, 13, "V5", 15, 16,
)
VEC_PATH = "c012y"
ROWS_VEC = 16
CHUNK = 1024
ATTEND = 6


def unit_dims(unit, rows, width):
    kind = unit[0]
    if kind == "d":
        return None, unit[3], 128
    if kind == "u":
        return None, rows, unit[3]
    if kind == "o":
        return None, rows, width
    return unit[2], rows, 256


def land_shape(unit, path, stage, rows, width):
    many, r, c = unit_dims(unit, rows, width)
    lead = [2, 2, 2]
    for kind in path[: stage + 1]:
        if kind == "c" and unit[0] != "d":
            c //= 2
        elif kind in "cy":
            r //= 2
        elif kind != "Y":
            lead[2 - int(kind)] = 0
    return (() if many is None else (many,)) + tuple(n for n in lead if n) + (r, c)


def gelu_parts(x):
    cdf = 0.5 + 0.5 * lax.erf(x * (0.5**0.5))
    pdf = jnp.exp(-0.5 * x * x) * 0.3989422804014327
    return x * cdf, cdf + x * pdf


def layer_kernel(*refs):
    it = iter(refs)
    len_ref = next(it)
    bias_refs = [next(it) for _ in range(9)]
    (tok_ref, cot_ref, wq_ref, wk_ref, wv_ref, wo_ref, wu_ref, wd_ref) = (next(it) for _ in range(8))
    (mix_out, dtok_out, go_out, gp_out, gu_out, gd_out, gv_out) = (next(it) for _ in range(7))
    (raw_s, tokp, cotp, x_s, cot_s, x_t, hl_t, df_t) = (next(it) for _ in range(8))
    (wa, wu, wd, gd_s, qkv_s, p_s, att_s, linv_s, xh_s, rs_s, hl_s, act_s, gp_s, acc_s, km_s, vec_s) = (
        next(it) for _ in range(16)
    )
    vs, vl = next(it), next(it)
    lands = [[next(it) for _ in path] for path in PATH]
    tails = [next(it) if "y" in path else None for path in PATH]
    (wsem, lsem, asend, arecv, usend, urecv, vsend, vrecv) = (next(it) for _ in range(8))

    rows_loc, width = tok_ref.shape[0], tok_ref.shape[2]
    total = rows_loc * 4
    half = total // 2
    rows = width // 8
    dp, sp = lax.axis_index("dp"), lax.axis_index("sp")
    bits = [lax.rem(lax.div(dp, 2**k), 2) for k in range(3)]
    core, ybit = lax.rem(sp, 2), lax.div(sp, 2)

    def sp_xor(k):
        low, high = core, ybit
        if k & 1:
            low = 1 - low
        if k & 2:
            high = 1 - high
        return high * 2 + low

    def peer(kind):
        if kind == "c":
            return (dp, sp_xor(1))
        if kind in "yY":
            return (dp, sp_xor(2))
        k = int(kind)
        return (dp + 2**k * (1 - 2 * bits[k]), sp)

    barrier = pltpu.get_barrier_semaphore()
    greet = [(dp, sp_xor(k)) for k in (1, 2, 3)] + [peer(k) for k in "012"]
    for other in greet:
        pl.semaphore_signal(barrier, inc=1, device_id=other, device_id_type=MESH_ID)

    loads = []

    def load(src, dst):
        copy = pltpu.make_async_copy(src, dst, wsem.at[len(loads)])
        copy.start()
        loads.append(copy)
        return copy

    quick = rows_loc // 2
    tok_loads = [load(tok_ref.at[pl.ds(i * quick, quick)], raw_s.at[pl.ds(i * quick, quick)]) for i in range(2)]
    attn_loads = [load(ref, wa.at[i]) for i, ref in enumerate((wq_ref, wk_ref, wv_ref, wo_ref))]

    def exchange(src, dst, base, first=0, size=rows_loc):
        copies = []
        for k in (2, 3, 1):
            other = sp_xor(k)
            copy = pltpu.make_async_remote_copy(
                src_ref=src.at[other, pl.ds(first, size)],
                dst_ref=dst.at[pl.ds(aligned(sp * rows_loc + first, size), size)],
                send_sem=asend.at[base + k - 1],
                recv_sem=arecv.at[base + k - 1],
                device_id=(dp, other),
                device_id_type=MESH_ID,
            )
            copy.start()
            copies.append(copy)
        dst[pl.ds(aligned(sp * rows_loc + first, size), size), :] = src[sp, pl.ds(first, size)]
        return copies

    tok_copies = []
    for i in range(2):
        tok_loads[i].wait()
        tokp[:, pl.ds(i * quick, quick)] = jnp.swapaxes(raw_s[pl.ds(i * quick, quick)], 0, 1)
        if i == 0:
            pl.semaphore_wait(barrier, len(greet))
        tok_copies += exchange(tokp, x_s, 12 * i, i * quick, quick)
    cot_load = load(cot_ref, raw_s)
    up_loads = [
        [load(wu_ref.at[:, :, :, :, pl.ds(384 * r + 128 * j, 128)], wu.at[j, :, :, :, :, pl.ds(128 * r, 128)]) for r in range(8)]
        for j in range(3)
    ]
    down_loads = [load(wd_ref.at[:, :, :, j], wd.at[j]) for j in range(3)]

    vec_s[1:2, :] = jnp.zeros((1, CHUNK), F32)
    for i, row in enumerate((0, 2, 3, 4, 5, 6, 7, 8)):
        vec_s[pl.ds(row, 1), pl.ds(0, width)] = bias_refs[i][...].astype(F32).reshape(1, width)
    for j in range(3):
        for r in range(8):
            part = bias_refs[8][pl.ds(384 * r + 128 * j, 128)]
            vec_s[pl.ds(10 + j, 1), pl.ds(128 * r, 128)] = part.astype(F32).reshape(1, 128)

    state = [dict(stage=0, copies=[]) for _ in UNITS]

    def region(unit, kinds, last_other=False, at_y=None):
        kind = unit[0]
        many, r, c = unit_dims(unit, rows, width)
        r0, c0 = (unit[2] if kind == "d" else 0), (256 * unit[3] if kind == "p" else unit[2] if kind == "u" else 0)
        lead = [slice(None)] * 3
        for i, step in enumerate(kinds):
            flip = last_other and i == len(kinds) - 1
            if step == "c":
                at = 1 - core if flip else core
                if kind == "d":
                    r //= 2
                    r0 = r0 + at * r
                else:
                    c //= 2
                    c0 = c0 + at * c
            elif step == "y":
                r //= 2
                r0 = r0 + (1 - ybit if flip else ybit if at_y is None else at_y) * r
            elif step != "Y":
                b = bits[int(step)]
                lead[2 - int(step)] = 1 - b if flip else b
        span = (pl.ds(r0 if isinstance(r0, int) else aligned(r0, 16), r), pl.ds(c0 if isinstance(c0, int) else aligned(c0), c))
        if kind == "d":
            return gd_s, (unit[1], *lead, *span)
        if kind == "u":
            return wu, (unit[1], *lead, *span)
        if kind == "o":
            return wa, (3, *lead, *span)
        return wd, (pl.ds(unit[1], many), *lead, *span)

    def out_region(unit, path, at_y=None):
        ref, at = region(unit, path, at_y=at_y)
        kind = unit[0]
        if kind == "d":
            return gd_out.at[unit[1], at[4], at[5]]
        if kind == "u":
            return gu_out.at[unit[1], at[4], at[5]]
        if kind == "o":
            return go_out.at[at[4], at[5]]
        return gp_out.at[at[0], at[4], at[5]]

    def send(n, stage, src, dst, to):
        copy = pltpu.make_async_remote_copy(
            src_ref=src,
            dst_ref=dst,
            send_sem=usend.at[n, stage],
            recv_sem=urecv.at[n, stage],
            device_id=to,
            device_id_type=MESH_ID,
        )
        copy.start()
        state[n]["copies"].append(copy)

    def advance(n):
        unit, path = UNITS[n], PATH[n]
        stage = state[n]["stage"]
        state[n]["stage"] += 1
        if stage > len(path):
            state[n]["copies"][stage - 1].wait_recv()
            dst = out_region(unit, path, 1 - ybit)
            send(n, stage + 1, tails[n], dst, peer("c"))
            local = pltpu.make_async_copy(tails[n], dst, lsem.at[n, 1])
            local.start()
            state[n]["local"].append(local)
            return
        if stage > 0:
            state[n]["copies"][stage - 1].wait_recv()
            ref, at = region(unit, path[:stage])
            if path[stage - 1] == "Y":
                lands[n][stage - 1][...] = ref[at] + lands[n][stage - 1][...]
            else:
                ref[at] = ref[at] + lands[n][stage - 1][...]
        if stage < len(path):
            ref, at = region(unit, path[: stage + 1], last_other=True)
            send(n, stage, ref.at[at], lands[n][stage], peer(path[stage]))
            return
        dst = out_region(unit, path)
        if "Y" in path:
            src = lands[n][-1]
            send(n, stage, src, dst, peer("c"))
        else:
            ref, at = region(unit, path)
            src = ref.at[at]
            send(n, stage, src, tails[n], peer("y"))
            send(n, stage + 1, src, dst, peer("c"))
        local = pltpu.make_async_copy(src, dst, lsem.at[n, 0])
        local.start()
        state[n]["local"] = [local]

    def finish(n):
        for copy in state[n]["copies"][len(PATH[n]) + ("y" in PATH[n]) :]:
            copy.wait_recv()
        for copy in state[n]["copies"]:
            copy.wait_send()
        for copy in state[n]["local"]:
            copy.wait()

    def vec(row):
        return vec_s[pl.ds(row, 1), pl.ds(0, width)]

    def put_vec(row, value):
        vs[0, pl.ds(row, 1), pl.ds(0, value.shape[1])] = value

    vs[0] = jnp.zeros(vs.shape[1:], F32)
    length = len_ref[sp]
    dead = lax.broadcasted_iota(jnp.int32, (total, 128), 0) >= length
    km_s[...] = jnp.where(dead, -1e30, 0.0).astype(BF)
    ones = jnp.ones((16, total), BF)
    for ref in (x_t, hl_t, df_t):
        ref[pl.ds(width, 16), :] = ones

    def qkv(start):
        def one(w, carry):
            r = nn(x_s[pl.ds(start, half), :], wa[w].reshape(width, width)) + vec_s[pl.ds(w, 1), pl.ds(0, width)]
            r = r * jnp.where(w == 0, HD ** (-0.5), 1.0)
            qkv_s[w, pl.ds(start, half), :] = r.astype(BF)
            return carry

        lax.fori_loop(0, 3, one, 0)

    for copy in attn_loads[:3]:
        copy.wait()
    for i in (2, 5):
        tok_copies[i].wait_recv()
    qkv(aligned(ybit * half))
    cot_load.wait()
    cotp[...] = jnp.swapaxes(raw_s[...], 0, 1)
    for i in (0, 1, 3, 4):
        tok_copies[i].wait_recv()
    cot_copies = exchange(cotp, cot_s, 3)
    qkv(aligned((1 - ybit) * half))

    lane = lax.broadcasted_iota(jnp.int32, (total, 128), 1)
    low = lane < HD
    zeros = jnp.zeros((total, 128), BF)
    ones2 = jnp.ones((total, 128), BF)

    def attend(g):
        cols = pl.ds(aligned(g * 128), 128)
        q2, k2, v2 = qkv_s[0, :, cols], qkv_s[1, :, cols], qkv_s[2, :, cols]
        outs = []
        for h in range(2):
            mine = low if h == 0 else jnp.logical_not(low)
            qh = jnp.where(mine, q2, jnp.where(lane == HD * (1 - h), ones2, zeros))
            kh = jnp.where(mine, k2, km_s[...])
            vh = jnp.where(mine, v2, ones2)
            s = nt(qh, kh)
            e = jnp.exp(s - jnp.max(s, axis=-1, keepdims=True)).astype(BF)
            p_s[g * 2 + h] = e
            outs.append(nn(e, vh))
        num = jnp.where(low, outs[0], outs[1])
        den = pltpu.roll(jnp.where(low, outs[1], outs[0]), HD, axis=1)
        inv = 1.0 / den
        linv_s[:, cols] = inv.astype(BF)
        att_s[:, cols] = (num * inv).astype(BF)

    def attend_some(i, carry):
        for g in range(ATTEND):
            attend(i * ATTEND + g)
        return carry

    lax.fori_loop(0, HEADS // 2 // ATTEND, attend_some, 0)

    attn_loads[3].wait()

    def first_norm(i, carry):
        at = pl.ds(aligned(256 * i, 256), 256)
        r = nn(att_s[at, :], wa[3].reshape(width, width)) + vec(3) + x_s[at, :].astype(F32)
        mean = jnp.mean(r, axis=-1, keepdims=True)
        center = r - mean
        rs = lax.rsqrt(jnp.mean(center * center, axis=-1, keepdims=True) + EPS)
        xh = center * rs
        hidden = xh * vec(4) + vec(5)
        rs_s[at, :] = rs
        xh_s[at, :] = xh.astype(BF)
        acc_s[at, :] = hidden
        hl_s[at, :] = hidden.astype(BF)
        return carry

    lax.fori_loop(0, total // 256, first_norm, 0)

    for j in range(3):
        for copy in up_loads[j]:
            copy.wait()

    def up(j, carry):
        inner = nn(hl_s[...], wu[j].reshape(width, CHUNK)) + vec_s[pl.ds(10 + j, 1), :]
        value, slope = gelu_parts(inner)
        act_s[j] = value.astype(BF)
        gp_s[j] = slope.astype(BF)
        return carry

    lax.fori_loop(0, 3, up, 0)

    for copy in down_loads:
        copy.wait()

    def down(i, carry):
        cols = pl.ds(aligned(i * 256), 256)
        r = acc_s[:, cols] + vec_s[pl.ds(6, 1), cols]
        for j in range(3):
            r = r + nn(act_s[j], wd[j, :, :, :, :, cols].reshape(CHUNK, 256))
        acc_s[:, cols] = r
        return carry

    lax.fori_loop(0, width // 256, down, 0)

    for copy in cot_copies:
        copy.wait_recv()
    for copy in tok_copies + cot_copies:
        copy.wait_send()

    def second_norm(i, carry):
        at = pl.ds(aligned(128 * i, 128), 128)
        r = acc_s[at, :]
        mean = jnp.mean(r, axis=-1, keepdims=True)
        center = r - mean
        rs = lax.rsqrt(jnp.mean(center * center, axis=-1, keepdims=True) + EPS)
        xh = center * rs
        tokp[i] = (xh * vec(7) + vec(8)).astype(BF)
        dy = cot_s[at, :].astype(F32)
        dxh = dy * vec(7)
        d2 = rs * (dxh - jnp.mean(dxh, axis=-1, keepdims=True) - xh * jnp.mean(dxh * xh, axis=-1, keepdims=True))
        acc_s[at, :] = d2
        low2 = d2.astype(BF)
        cot_s[at, :] = low2
        df_t[:width, at] = low2.T
        adds = (
            jnp.sum(dy * xh, axis=0, keepdims=True),
            jnp.sum(dy, axis=0, keepdims=True),
            jnp.sum(low2.astype(F32), axis=0, keepdims=True),
        )
        return tuple(c + a for c, a in zip(carry, adds))

    zero = jnp.zeros((1, width), F32)
    g_gain, g_shift, g_bdown = lax.fori_loop(0, total // 128, second_norm, (zero, zero, zero))
    put_vec(6, g_gain)
    put_vec(7, g_shift)
    put_vec(5, g_bdown)

    given = []

    def give_back(src, dst, base):
        for k in (2, 3, 1):
            other = sp_xor(k)
            copy = pltpu.make_async_remote_copy(
                src_ref=src.at[other],
                dst_ref=dst.at[sp],
                send_sem=asend.at[base + k - 1],
                recv_sem=arecv.at[base + k - 1],
                device_id=(dp, other),
                device_id_type=MESH_ID,
            )
            copy.start()
            given.append(copy)
        own = pltpu.make_async_copy(src.at[sp], dst.at[sp], lsem.at[len(UNITS) + base // 3 - 2, 0])
        own.start()
        given.append(own)

    def grad_down(j, first, size):
        r = nn(df_t[pl.ds(first, size), :], act_s[j]).astype(BF)
        for k in range(8):
            gd_s[j, k // 4, k // 2 % 2, k % 2, pl.ds(first, size), :] = r[:, 128 * k : 128 * k + 128]

    def inner_back(first, count):
        def body(j, carry):
            gp_s[j] = nt(cot_s[...], wd[j].reshape(CHUNK, width)).astype(BF) * gp_s[j]
            return carry

        lax.fori_loop(first, first + count, body, 0)

    def hidden_back(first, count):
        def body(j, carry):
            acc_s[...] += nt(gp_s[j], wu[j].reshape(width, CHUNK))
            return carry

        lax.fori_loop(first, first + count, body, 0)

    def grad_up(first, count):
        def body(j, carry):
            r = nn(hl_t[...], gp_s[j])
            wu[j] = r[:width].astype(BF).reshape(2, 2, 2, rows, CHUNK)
            vs[0, pl.ds(10 + j, 1), :] = r[width : width + 1]
            return carry

        lax.fori_loop(first, first + count, body, 0)

    def first_back():
        def body(i, carry):
            at = pl.ds(aligned(128 * i, 128), 128)
            dy = acc_s[at, :]
            xh = xh_s[at, :].astype(F32)
            dxh = dy * vec(4)
            d1 = rs_s[at, :] * (
                dxh - jnp.mean(dxh, axis=-1, keepdims=True) - xh * jnp.mean(dxh * xh, axis=-1, keepdims=True)
            )
            acc_s[at, :] = d1
            dh_s[at, :] = d1.astype(BF)
            adds = (jnp.sum(dy * xh, axis=0, keepdims=True), jnp.sum(dy, axis=0, keepdims=True))
            return tuple(c + a for c, a in zip(carry, adds))

        g_gain, g_shift = lax.fori_loop(0, total // 128, body, (zero, zero))
        put_vec(3, g_gain)
        put_vec(4, g_shift)

    def attended_back():
        d = nt(dh_s[...], wa[3].reshape(width, width))
        da_s[...] = (d * linv_s[...].astype(F32)).astype(BF)

    da_s = linv_s

    def grad_out():
        df_t[:width, :] = att_s[...].T
        r = nn(df_t[...], dh_s[...])
        wa[3] = r[:width].astype(BF).reshape(2, 2, 2, rows, width)
        vs[0, 2:3, :width] = r[width : width + 1]

    def attend_back(g):
        cols = slice(g * 128, g * 128 + 128)
        q2, k2, v2, d2 = qkv_s[0, :, cols], qkv_s[1, :, cols], qkv_s[2, :, cols], da_s[:, cols]
        prod = d2.astype(F32) * att_s[:, cols].astype(F32)
        dqs, dks, dvs = [], [], []
        for h in range(2):
            mine = low if h == 0 else jnp.logical_not(low)
            delta = -jnp.sum(jnp.where(mine, prod, 0.0), axis=-1, keepdims=True)
            upper = delta.astype(BF)
            lower = (delta - upper.astype(F32)).astype(BF)
            other = HD * (1 - h)
            fill = jnp.where(lane == other, upper, jnp.where(lane == other + 1, lower, zeros))
            e = p_s[g * 2 + h]
            ds = e * nt(jnp.where(mine, d2, fill), jnp.where(mine, v2, ones2)).astype(BF)
            dqs.append(nn(ds, k2))
            dks.append(tn(ds, q2))
            dvs.append(tn(e, d2))
        qkv_s[0, :, cols] = (jnp.where(low, dqs[0], dqs[1]) * HD ** (-0.5)).astype(BF)
        qkv_s[1, :, cols] = jnp.where(low, dks[0], dks[1]).astype(BF)
        qkv_s[2, :, cols] = jnp.where(low, dvs[0], dvs[1]).astype(BF)

    def grad_proj(n):
        cols = slice(256 * n, 256 * n + 256)

        def body(w, carry):
            r = nn(x_t[...], qkv_s[w, :, cols])
            wd[w, :, :, :, :rows, cols] = r[:width].astype(BF).reshape(2, 2, 2, rows, 256)
            vs[0, pl.ds(lax.rem(w * 14, 27), 1), cols] = r[width : width + 1]
            return carry

        lax.fori_loop(0, 3, body, 0)

    def tokens_back():
        def body(w, carry):
            acc_s[...] += nt(qkv_s[w], wa[w].reshape(width, width))
            return carry

        lax.fori_loop(0, 3, body, 0)
        cotp[...] = acc_s[...].astype(BF).reshape(4, rows_loc, width)

    vec_copies = []

    def vec_step(i):
        if i == 0:
            vl[0] = vs[0].astype(BF)
        else:
            vec_copies[i - 1].wait_recv()
            vl[i] = vl[i - 1] + vl[i]
        if i < 5:
            copy = pltpu.make_async_remote_copy(
                src_ref=vl.at[i],
                dst_ref=vl.at[i + 1],
                send_sem=vsend.at[i],
                recv_sem=vrecv.at[i],
                device_id=peer(VEC_PATH[i]),
                device_id_type=MESH_ID,
            )
            copy.start()
            vec_copies.append(copy)

    def transpose_tokens():
        x_t[:width, :] = x_s[...].T
        hl_t[:width, :] = hl_s[...].T

    dh_s = hl_s

    made = set()

    def produce(n):
        unit = UNITS[n]
        if unit[0] == "d" and unit[1] == 0:
            grad_down(0, unit[2], unit[3])
            return
        key = (unit[0], unit[3]) if unit[0] == "p" else (unit[0], min(unit[1], 1)) if unit[0] in "du" else unit
        if key in made:
            return
        made.add(key)
        if key == ("d", 1):

            def both(j, carry):
                grad_down(j, 0, width)
                return carry

            lax.fori_loop(1, 3, both, 0)
        elif key[0] == "u":
            grad_up(key[1], 1 + key[1])
        elif key[0] == "o":
            grad_out()
        else:
            grad_proj(unit[3])

    for step in ORDER:
        if isinstance(step, int):
            if state[step]["stage"] == 0:
                produce(step)
            advance(step)
            continue
        name, at = step[0], int(step[1:] or 0)
        if name == "I":
            inner_back(at, 1 + at)
        elif name == "H":
            hidden_back(at, 3)
        elif name == "F":
            first_back()
        elif name == "A":
            attended_back()
        elif name == "B":
            attend_back(at)
            attend_back(at + 1)
        elif name == "T":
            tokens_back()
        elif name == "X":
            transpose_tokens()
        elif name == "M":
            give_back(tokp, mix_out, 6)
        elif name == "K":
            give_back(cotp, dtok_out, 9)
        elif name == "V":
            vec_step(at)
    gv_out[...] = vl[5].astype(F32)
    for n in range(len(UNITS)):
        finish(n)
    for copy in vec_copies:
        copy.wait_send()
    for copy in given:
        copy.wait()


def finish_kernel(*refs):
    it = iter(refs)
    sources = [next(it) for _ in range(7)]
    (o_mix, o_dtok, o_wq, o_bq, o_wk, o_wv, o_bv, o_wo, o_bo, o_ga, o_sa, o_up, o_bup, o_down, o_bdown, o_gf, o_sf) = (
        next(it) for _ in range(17)
    )
    held = [next(it) for _ in range(7)]
    staged = [next(it) for _ in range(5)]
    isem, osem = next(it), next(it)
    loads = [pltpu.make_async_copy(src, dst, isem.at[i]) for i, (src, dst) in enumerate(zip(sources, held))]
    for copy in loads:
        copy.start()
    mix, dtok, go, gp, gu, gd, gv = held
    s_mix, s_dtok, s_sq, s_up, s_down = staged
    width = mix.shape[2]
    rows = width // 8
    dp = lax.axis_index("dp")
    stores = []

    def store(src, dst):
        copy = pltpu.make_async_copy(src, dst, osem.at[len(stores)])
        copy.start()
        stores.append(copy)

    loads[4].wait()
    for j in range(3):
        for r in range(8):
            s_up[:, 384 * r + 128 * j : 384 * r + 128 * j + 128] = gu[j, :, 128 * r : 128 * r + 128].astype(F32)
    store(s_up, o_up)
    loads[5].wait()
    for j in range(3):
        s_down[128 * j : 128 * j + 128, :] = gd[j].astype(F32).T
    store(s_down, o_down)
    loads[3].wait()
    loads[2].wait()
    for w in range(4):
        s_sq[w] = (go[...] if w == 3 else gp[w]).astype(F32)
        store(s_sq.at[w], (o_wq, o_wk, o_wv, o_wo)[w])
    loads[0].wait()
    s_mix[...] = jnp.swapaxes(mix[...], 0, 1)
    store(s_mix, o_mix)
    loads[1].wait()
    s_dtok[...] = jnp.swapaxes(dtok[...], 0, 1)
    store(s_dtok, o_dtok)
    loads[6].wait()
    for j in range(3):
        o_bup[pl.ds(128 * j, 128)] = gv[pl.ds(10 + j, 1), pl.ds(aligned(dp * 128), 128)].reshape(128)
    turned = pltpu.roll(gv[pl.ds(0, 8), pl.ds(0, width)], lax.rem(width - rows * dp, width), axis=1)
    for i, ref in enumerate((o_bq, o_bv, o_bo, o_ga, o_sa, o_bdown, o_gf, o_sf)):
        ref[...] = turned[i : i + 1, :rows].reshape(rows)
    for copy in stores:
        copy.wait()


def fused(
    tokens, lengths, w_query, b_query, w_key, w_value, b_value, w_out, b_out, gain_attn, shift_attn,
    w_up, b_up, w_down, b_down, gain_ffn, shift_ffn, cotangent,
):
    rows_loc, pairs, width = tokens.shape
    total = rows_loc * 4
    rows = width // 8
    square = lambda w: w.reshape(2, 2, 2, rows, w.shape[1])
    args = (
        lengths, b_query, b_value, b_out, gain_attn, shift_attn, b_down, gain_ffn, shift_ffn, b_up, tokens, cotangent,
        square(w_query), square(w_key), square(w_value), square(w_out), square(w_up),
        w_down.reshape(2, 2, 2, 3, 128, width),
    )
    vm = lambda shape, dtype=BF: pltpu.VMEM(shape, dtype)
    full = (total, width)
    swapped = (4, rows_loc, width)
    turned = (width + 16, total)
    scratch = [
        vm((rows_loc, 4, width)), vm(swapped), vm(swapped), vm(full), vm(full), vm(turned), vm(turned), vm(turned),
        vm((4, 2, 2, 2, rows, width)), vm((3, 2, 2, 2, rows, CHUNK)), vm((3, 2, 2, 2, 128, width)),
        vm((3, 2, 2, 2, width, 128)),
        vm((3, total, width)), vm((HEADS, total, total)), vm(full), vm(full),
        vm(full), vm((total, 1), F32), vm(full), vm((3, total, CHUNK)), vm((3, total, CHUNK)),
        vm(full, F32), vm((total, 128)), vm((ROWS_VEC, CHUNK), F32),
        vm((1, ROWS_VEC, CHUNK), F32), vm((6, ROWS_VEC, CHUNK)),
    ]
    for unit, path in zip(UNITS, PATH):
        scratch += [vm(land_shape(unit, path, s, rows, width)) for s in range(len(path))]
    for unit, path in zip(UNITS, PATH):
        if "y" in path:
            scratch.append(vm(land_shape(unit, path, 4, rows, width)))
    dma = pltpu.SemaphoreType.DMA
    count = len(UNITS)
    scratch += [dma((40,)), dma((count + 2, 2)), dma((15,)), dma((15,)), dma((count, 8)), dma((count, 8)), dma((5,)), dma((5,))]
    anywhere = pl.BlockSpec(memory_space=pl.ANY)
    vmem = pl.BlockSpec(memory_space=pltpu.VMEM)
    got = pl.pallas_call(
        layer_kernel,
        out_shape=(
            jax.ShapeDtypeStruct(swapped, BF),
            jax.ShapeDtypeStruct(swapped, BF),
            jax.ShapeDtypeStruct((rows, width), BF),
            jax.ShapeDtypeStruct((3, rows, width), BF),
            jax.ShapeDtypeStruct((3, rows, CHUNK), BF),
            jax.ShapeDtypeStruct((3, width, 128), BF),
            jax.ShapeDtypeStruct((ROWS_VEC, CHUNK), F32),
        ),
        in_specs=[pl.BlockSpec(memory_space=pltpu.SMEM)] + [vmem] * 9 + [anywhere] * 8,
        out_specs=(anywhere,) * 6 + (vmem,),
        scratch_shapes=scratch,
        compiler_params=pltpu.CompilerParams(collective_id=0, has_side_effects=True, vmem_limit_bytes=63 * 2**20),
    )(*args)
    small = jax.ShapeDtypeStruct((rows,), F32)
    flat = jax.ShapeDtypeStruct((rows, width), F32)
    whole = jax.ShapeDtypeStruct((rows_loc, 4, width), BF)
    return pl.pallas_call(
        finish_kernel,
        out_shape=(
            whole, whole, flat, small, flat, flat, small, flat, small, small, small,
            jax.ShapeDtypeStruct((rows, 3 * CHUNK), F32),
            jax.ShapeDtypeStruct((384,), F32),
            jax.ShapeDtypeStruct((384, width), F32),
            small, small, small,
        ),
        in_specs=[anywhere] * 7,
        out_specs=tuple(anywhere if big else vmem for big in (1, 1, 1, 0, 1, 1, 0, 1, 0, 0, 0, 1, 0, 1, 0, 0, 0)),
        scratch_shapes=[vm(value.shape, value.dtype) for value in got]
        + [
            vm((rows_loc, 4, width)), vm((rows_loc, 4, width)), vm((4, rows, width), F32),
            vm((rows, 3 * CHUNK), F32), vm((384, width), F32), dma((7,)), dma((8,)),
        ],
        compiler_params=pltpu.CompilerParams(vmem_limit_bytes=63 * 2**20),
    )(*got)


def norm_layer(resid, gain, shift):
    center = resid - jnp.mean(resid, axis=-1, keepdims=True)
    spread = jnp.mean(center * center, axis=-1, keepdims=True)
    return center * lax.rsqrt(spread + 1e-05) * gain + shift


def exact_gelu(value):
    return jax.nn.gelu(value, approximate=False)


def project(left, weight):
    return jnp.einsum("spd,de->spe", left, weight, preferred_element_type=jnp.float32)


def back_project(grad_in, weight):
    return jnp.einsum("spe,de->spd", grad_in, weight, preferred_element_type=jnp.float32)


def weight_grad(left, right):
    return jnp.einsum("spd,spe->de", left, right, preferred_element_type=jnp.float32)


def column_sum(grad_in):
    return jnp.sum(grad_in.astype(jnp.float32), axis=(0, 1))


def shards(
    tokens,
    lengths,
    w_query,
    b_query,
    w_key,
    w_value,
    b_value,
    w_out,
    b_out,
    gain_attn,
    shift_attn,
    w_up,
    b_up,
    w_down,
    b_down,
    gain_ffn,
    shift_ffn,
    cotangent,
):
    local_rows, pair_count, model_width = tokens.shape
    score_scale = HD ** (-0.5)
    total_len = local_rows * lax.axis_size("sp")
    queries = (project(tokens, w_query) + b_query.astype(jnp.float32)).astype(jnp.bfloat16)
    keys_local = project(tokens, w_key).astype(jnp.bfloat16)
    values_local = (project(tokens, w_value) + b_value.astype(jnp.float32)).astype(jnp.bfloat16)
    keys_all, values_all = (
        lax.all_gather(keys_local, "sp", axis=0, tiled=True),
        lax.all_gather(values_local, "sp", axis=0, tiled=True),
    )
    query_heads = queries.reshape(local_rows, pair_count, HEADS, HD)
    key_heads = keys_all.reshape(total_len, pair_count, HEADS, HD)
    value_heads = values_all.reshape(total_len, pair_count, HEADS, HD)
    scores = (
        jnp.einsum("iphe,jphe->phij", query_heads, key_heads, preferred_element_type=jnp.float32)
        * score_scale
    )
    key_valid = jnp.arange(total_len)[None, :] < lengths[:, None]
    scores = jnp.where(key_valid[:, None, None, :], scores, -1e30)
    top_score = jnp.max(scores, axis=-1, keepdims=True)
    expo = jnp.exp(scores - top_score)
    row_total = jnp.sum(expo, axis=-1, keepdims=True)
    weights_full = expo / row_total
    probs = weights_full.astype(jnp.bfloat16)
    attended = jnp.einsum("phij,jphe->iphe", probs, value_heads, preferred_element_type=jnp.float32)
    attended_low = attended.reshape(local_rows, pair_count, model_width).astype(jnp.bfloat16)
    branch = project(attended_low, w_out) + b_out.astype(jnp.float32)
    first_sum = tokens.astype(jnp.float32) + branch
    hidden, first_back = jax.vjp(
        norm_layer, first_sum, gain_attn.astype(jnp.float32), shift_attn.astype(jnp.float32)
    )
    hidden_low = hidden.astype(jnp.bfloat16)
    inner = project(hidden_low, w_up) + b_up.astype(jnp.float32)
    activated, gelu_back = jax.vjp(exact_gelu, inner)
    activated_low = activated.astype(jnp.bfloat16)
    second_sum = hidden + project(activated_low, w_down) + b_down.astype(jnp.float32)
    mixed, second_back = jax.vjp(
        norm_layer, second_sum, gain_ffn.astype(jnp.float32), shift_ffn.astype(jnp.float32)
    )
    d_second, grad_gain_ffn, grad_shift_ffn = second_back(cotangent.astype(jnp.float32))
    d_ffn = d_second.astype(jnp.bfloat16)
    grad_down = weight_grad(activated_low, d_ffn)
    grad_bdown = column_sum(d_ffn)
    d_inner = gelu_back(back_project(d_ffn, w_down))[0].astype(jnp.bfloat16)
    grad_up = weight_grad(hidden_low, d_inner)
    grad_bup = column_sum(d_inner)
    d_hidden = d_second + back_project(d_inner, w_up)
    d_first, grad_gain_attn, grad_shift_attn = first_back(d_hidden)
    d_branch = d_first.astype(jnp.bfloat16)
    grad_out = weight_grad(attended_low, d_branch)
    grad_bout = column_sum(d_branch)
    d_attended = back_project(d_branch, w_out).astype(jnp.bfloat16)
    d_att_heads = d_attended.reshape(local_rows, pair_count, HEADS, HD)
    d_probs = jnp.einsum(
        "iphe,jphe->phij", d_att_heads, value_heads, preferred_element_type=jnp.float32
    )
    row_delta = jnp.sum(weights_full * d_probs, axis=-1, keepdims=True)
    d_scores = weights_full * (d_probs - row_delta)
    d_scores_low = d_scores.astype(jnp.bfloat16)
    d_query_heads = (
        jnp.einsum("phij,jphe->iphe", d_scores_low, key_heads, preferred_element_type=jnp.float32)
        * score_scale
    )
    d_queries = d_query_heads.reshape(local_rows, pair_count, model_width).astype(jnp.bfloat16)
    row_count = local_rows * lax.axis_size("sp")
    key_part = (
        jnp.einsum("phij,iphe->jphe", d_scores_low, query_heads, preferred_element_type=jnp.float32)
        * score_scale
    )
    value_part = jnp.einsum(
        "phij,iphe->jphe", probs, d_att_heads, preferred_element_type=jnp.float32
    )
    key_grads = lax.psum_scatter(
        jnp.concatenate(
            (
                key_part.reshape(row_count, pair_count, model_width),
                value_part.reshape(row_count, pair_count, model_width),
            ),
            axis=2,
        ).astype(jnp.bfloat16),
        "sp",
        scatter_dimension=0,
        tiled=True,
    ).astype(jnp.float32)
    d_keys = key_grads[:, :, :model_width].astype(jnp.bfloat16)
    d_values = key_grads[:, :, model_width:].astype(jnp.bfloat16)
    grad_query = weight_grad(tokens, d_queries)
    grad_bquery = column_sum(d_queries)
    grad_key = weight_grad(tokens, d_keys)
    grad_value = weight_grad(tokens, d_values)
    grad_bvalue = column_sum(d_values)
    d_tokens = (
        d_first
        + back_project(d_queries, w_query)
        + back_project(d_keys, w_key)
        + back_project(d_values, w_value)
    )
    summed = (
        lax.psum_scatter(grad_query, "dp", scatter_dimension=0, tiled=True),
        lax.psum_scatter(grad_bquery, "dp", scatter_dimension=0, tiled=True),
        lax.psum_scatter(grad_key, "dp", scatter_dimension=0, tiled=True),
        lax.psum_scatter(grad_value, "dp", scatter_dimension=0, tiled=True),
        lax.psum_scatter(grad_bvalue, "dp", scatter_dimension=0, tiled=True),
        lax.psum_scatter(grad_out, "dp", scatter_dimension=0, tiled=True),
        lax.psum_scatter(grad_bout, "dp", scatter_dimension=0, tiled=True),
        lax.psum_scatter(grad_gain_attn, "dp", scatter_dimension=0, tiled=True),
        lax.psum_scatter(grad_shift_attn, "dp", scatter_dimension=0, tiled=True),
        lax.psum_scatter(grad_up, "dp", scatter_dimension=0, tiled=True),
        lax.psum_scatter(grad_bup, "dp", scatter_dimension=0, tiled=True),
        lax.psum_scatter(grad_down, "dp", scatter_dimension=0, tiled=True),
        lax.psum_scatter(grad_bdown, "dp", scatter_dimension=0, tiled=True),
        lax.psum_scatter(grad_gain_ffn, "dp", scatter_dimension=0, tiled=True),
        lax.psum_scatter(grad_shift_ffn, "dp", scatter_dimension=0, tiled=True),
    )
    summed = tuple(
        (
            lax.psum(summed[0].astype(jnp.bfloat16), "sp").astype(jnp.float32),
            lax.psum(summed[1].astype(jnp.bfloat16), "sp").astype(jnp.float32),
            lax.psum(summed[2].astype(jnp.bfloat16), "sp").astype(jnp.float32),
            lax.psum(summed[3].astype(jnp.bfloat16), "sp").astype(jnp.float32),
            lax.psum(summed[4].astype(jnp.bfloat16), "sp").astype(jnp.float32),
            lax.psum(summed[5].astype(jnp.bfloat16), "sp").astype(jnp.float32),
            lax.psum(summed[6].astype(jnp.bfloat16), "sp").astype(jnp.float32),
            lax.psum(summed[7].astype(jnp.bfloat16), "sp").astype(jnp.float32),
            lax.psum(summed[8].astype(jnp.bfloat16), "sp").astype(jnp.float32),
            lax.psum(summed[9].astype(jnp.bfloat16), "sp").astype(jnp.float32),
            lax.psum(summed[10].astype(jnp.bfloat16), "sp").astype(jnp.float32),
            lax.psum(summed[11].astype(jnp.bfloat16), "sp").astype(jnp.float32),
            lax.psum(summed[12].astype(jnp.bfloat16), "sp").astype(jnp.float32),
            lax.psum(summed[13].astype(jnp.bfloat16), "sp").astype(jnp.float32),
            lax.psum(summed[14].astype(jnp.bfloat16), "sp").astype(jnp.float32),
        )
    )
    return (
        mixed.astype(jnp.bfloat16),
        d_tokens.astype(jnp.bfloat16),
        summed[0],
        summed[1],
        summed[2],
        summed[3],
        summed[4],
        summed[5],
        summed[6],
        summed[7],
        summed[8],
        summed[9],
        summed[10],
        summed[11],
        summed[12],
        summed[13],
        summed[14],
    )


def solution(mesh):
    placed = (
        P("sp", "dp", None),
        P("dp"),
        P(),
        P(),
        P(),
        P(),
        P(),
        P(),
        P(),
        P(),
        P(),
        P(),
        P(),
        P(),
        P(),
        P(),
        P(),
        P("sp", "dp", None),
    )
    fits = mesh.shape["dp"] == 8 and mesh.shape["sp"] == 4
    return jax.shard_map(
        fused if fits else shards,
        mesh=mesh,
        in_specs=placed,
        out_specs=(
            P("sp", "dp", None),
            P("sp", "dp", None),
            P("dp", None),
            P("dp"),
            P("dp", None),
            P("dp", None),
            P("dp"),
            P("dp", None),
            P("dp"),
            P("dp"),
            P("dp"),
            P("dp", None),
            P("dp"),
            P("dp", None),
            P("dp"),
            P("dp"),
            P("dp"),
        ),
        check_vma=False,
    )
```

profile of v0, /device:TPU:0, one launch (start us, length us, event | category | flops | bytes accessed | tf_op | source)
XLA Modules:
  0.0 112.7 jit_solution(6454866061033178391)
XLA Ops:
  0.7 107.0 %shard_map.305 = (bf16[4,128,768]{2,1,0:T(8,128)(2,1)}, bf16[4,128,768]{2,1,0:T(8,128)(2,1)}, bf16[96,768]{1,0:T(8,128)(2,1)}, bf16[3,96,768]{2,1,0:T(8,128)(2,1...) custom-call(s32[4]{0:T(128)} %refs_0_.1, bf16[768]{0:T(1024)(128)(2,1)} %refs_1_.1, ...), custom_call_target="tpu_custom_call" | custom-call | tf_op jit(solution)/shard_map/pallas_call | solution.py:718
  107.7 4.8 %shard_map.306 = (bf16[128,4,768]{2,1,0:T(4,128)(2,1)}, bf16[128,4,768]{2,1,0:T(4,128)(2,1)}, f32[96,768]{1,0:T(8,128)}, f32[96]{0:T(128)}, f32[96,768]{1,0:T(8,...) custom-call(bf16[4,128,768]{2,1,0:T(8,128)(2,1)} %get-tuple-element., ...), custom_call_target="tpu_custom_call" | custom-call | tf_op jit(solution)/shard_map/pallas_call | solution.py:737
where the time goes:
time: 113 us
  Pallas kernels  112 us (99%)
    pallas_call x1, Pallas kernels, fused(): pl.pallas_call(layer_kernel, out_shape=(jax.ShapeDtypeStruct(swapped, BF)...  107 us
    pallas_call x1, Pallas kernels, fused(): pl.pallas_call(finish_kernel, out_shape=(whole, whole, flat, small, flat,...  4.84 us

commit v1 on v0

--- a/solution.py
+++ b/solution.py
@@ -96,7 +96,7 @@
     vs, vl = next(it), next(it)
     lands = [[next(it) for _ in path] for path in PATH]
     tails = [next(it) if "y" in path else None for path in PATH]
-    (wsem, lsem, asend, arecv, usend, urecv, vsend, vrecv) = (next(it) for _ in range(8))
+    (wsem, lsem, asend, arecv, usend, urecv, ufin, vsend, vrecv) = (next(it) for _ in range(9))
 
     rows_loc, width = tok_ref.shape[0], tok_ref.shape[2]
     total = rows_loc * 4
@@ -127,48 +127,43 @@
     for other in greet:
         pl.semaphore_signal(barrier, inc=1, device_id=other, device_id_type=MESH_ID)
 
-    loads = []
-
-    def load(src, dst):
-        copy = pltpu.make_async_copy(src, dst, wsem.at[len(loads)])
+    def load(src, dst, at):
+        copy = pltpu.make_async_copy(src, dst, wsem.at[at])
         copy.start()
-        loads.append(copy)
         return copy
 
+    def landed(ref, sem):
+        pltpu.make_async_copy(ref, ref, sem).wait()
+
     quick = rows_loc // 2
-    tok_loads = [load(tok_ref.at[pl.ds(i * quick, quick)], raw_s.at[pl.ds(i * quick, quick)]) for i in range(2)]
-    attn_loads = [load(ref, wa.at[i]) for i, ref in enumerate((wq_ref, wk_ref, wv_ref, wo_ref))]
-
-    def exchange(src, dst, base, first=0, size=rows_loc):
-        copies = []
+    tok_loads = [load(tok_ref.at[pl.ds(i * quick, quick)], raw_s.at[pl.ds(i * quick, quick)], i) for i in range(2)]
+    attn_loads = [load(ref, wa.at[i], 2 + i) for i, ref in enumerate((wq_ref, wk_ref, wv_ref, wo_ref))]
+
+    def exchange(src, dst, group, first=0, size=rows_loc):
         for k in (2, 3, 1):
             other = sp_xor(k)
-            copy = pltpu.make_async_remote_copy(
+            pltpu.make_async_remote_copy(
                 src_ref=src.at[other, pl.ds(first, size)],
                 dst_ref=dst.at[pl.ds(aligned(sp * rows_loc + first, size), size)],
-                send_sem=asend.at[base + k - 1],
-                recv_sem=arecv.at[base + k - 1],
+                send_sem=asend.at[group],
+                recv_sem=arecv.at[2 if group else 0 if k == 1 else 1],
                 device_id=(dp, other),
                 device_id_type=MESH_ID,
-            )
-            copy.start()
-            copies.append(copy)
+            ).start()
         dst[pl.ds(aligned(sp * rows_loc + first, size), size), :] = src[sp, pl.ds(first, size)]
-        return copies
-
-    tok_copies = []
+
     for i in range(2):
         tok_loads[i].wait()
         tokp[:, pl.ds(i * quick, quick)] = jnp.swapaxes(raw_s[pl.ds(i * quick, quick)], 0, 1)
         if i == 0:
             pl.semaphore_wait(barrier, len(greet))
-        tok_copies += exchange(tokp, x_s, 12 * i, i * quick, quick)
-    cot_load = load(cot_ref, raw_s)
-    up_loads = [
-        [load(wu_ref.at[:, :, :, :, pl.ds(384 * r + 128 * j, 128)], wu.at[j, :, :, :, :, pl.ds(128 * r, 128)]) for r in range(8)]
-        for j in range(3)
-    ]
-    down_loads = [load(wd_ref.at[:, :, :, j], wd.at[j]) for j in range(3)]
+        exchange(tokp, x_s, 0, i * quick, quick)
+    cot_load = load(cot_ref, raw_s, 6)
+    for j in range(3):
+        for r in range(8):
+            load(wu_ref.at[:, :, :, :, pl.ds(384 * r + 128 * j, 128)], wu.at[j, :, :, :, :, pl.ds(128 * r, 128)], 7 + j)
+    for j in range(3):
+        load(wd_ref.at[:, :, :, j], wd.at[j], 10)
 
     vec_s[1:2, :] = jnp.zeros((1, CHUNK), F32)
     for i, row in enumerate((0, 2, 3, 4, 5, 6, 7, 8)):
@@ -221,12 +216,12 @@
             return go_out.at[at[4], at[5]]
         return gp_out.at[at[0], at[4], at[5]]
 
-    def send(n, stage, src, dst, to):
+    def send(n, stage, src, dst, to, last=False):
         copy = pltpu.make_async_remote_copy(
             src_ref=src,
             dst_ref=dst,
-            send_sem=usend.at[n, stage],
-            recv_sem=urecv.at[n, stage],
+            send_sem=usend.at[n],
+            recv_sem=ufin.at[0] if last else urecv.at[n, stage],
             device_id=to,
             device_id_type=MESH_ID,
         )
@@ -240,10 +235,8 @@
         if stage > len(path):
             state[n]["copies"][stage - 1].wait_recv()
             dst = out_region(unit, path, 1 - ybit)
-            send(n, stage + 1, tails[n], dst, peer("c"))
-            local = pltpu.make_async_copy(tails[n], dst, lsem.at[n, 1])
-            local.start()
-            state[n]["local"].append(local)
+            send(n, stage, tails[n], dst, peer("c"), last=True)
+            pltpu.make_async_copy(tails[n], dst, lsem.at[0]).start()
             return
         if stage > 0:
             state[n]["copies"][stage - 1].wait_recv()
@@ -259,23 +252,19 @@
         dst = out_region(unit, path)
         if "Y" in path:
             src = lands[n][-1]
-            send(n, stage, src, dst, peer("c"))
+            send(n, stage, src, dst, peer("c"), last=True)
         else:
             ref, at = region(unit, path)
             src = ref.at[at]
             send(n, stage, src, tails[n], peer("y"))
-            send(n, stage + 1, src, dst, peer("c"))
-        local = pltpu.make_async_copy(src, dst, lsem.at[n, 0])
-        local.start()
-        state[n]["local"] = [local]
+            send(n, stage, src, dst, peer("c"), last=True)
+        pltpu.make_async_copy(src, dst, lsem.at[0]).start()
 
     def finish(n):
-        for copy in state[n]["copies"][len(PATH[n]) + ("y" in PATH[n]) :]:
-            copy.wait_recv()
-        for copy in state[n]["copies"]:
-            copy.wait_send()
-        for copy in state[n]["local"]:
-            copy.wait()
+        many, r, c = unit_dims(UNITS[n], rows, width)
+        wide = (many or 1) * 8 * r * c // 256
+        cols = next(b for b in (512, 384, 256, 128) if wide % b == 0 and wide // b <= HEADS)
+        landed(p_s.at[pl.ds(0, wide // cols), pl.ds(0, 272), pl.ds(0, cols)], usend.at[n])
 
     def vec(row):
         return vec_s[pl.ds(row, 1), pl.ds(0, width)]
@@ -302,14 +291,12 @@
 
     for copy in attn_loads[:3]:
         copy.wait()
-    for i in (2, 5):
-        tok_copies[i].wait_recv()
+    landed(x_s.at[pl.ds(0, rows_loc)], arecv.at[0])
     qkv(aligned(ybit * half))
     cot_load.wait()
     cotp[...] = jnp.swapaxes(raw_s[...], 0, 1)
-    for i in (0, 1, 3, 4):
-        tok_copies[i].wait_recv()
-    cot_copies = exchange(cotp, cot_s, 3)
+    landed(x_s.at[pl.ds(0, half)], arecv.at[1])
+    exchange(cotp, cot_s, 1)
     qkv(aligned((1 - ybit) * half))
 
     lane = lax.broadcasted_iota(jnp.int32, (total, 128), 1)
@@ -362,8 +349,7 @@
     lax.fori_loop(0, total // 256, first_norm, 0)
 
     for j in range(3):
-        for copy in up_loads[j]:
-            copy.wait()
+        landed(wu.at[j], wsem.at[7 + j])
 
     def up(j, carry):
         inner = nn(hl_s[...], wu[j].reshape(width, CHUNK)) + vec_s[pl.ds(10 + j, 1), :]
@@ -374,8 +360,7 @@
 
     lax.fori_loop(0, 3, up, 0)
 
-    for copy in down_loads:
-        copy.wait()
+    landed(wd, wsem.at[10])
 
     def down(i, carry):
         cols = pl.ds(aligned(i * 256), 256)
@@ -387,10 +372,10 @@
 
     lax.fori_loop(0, width // 256, down, 0)
 
-    for copy in cot_copies:
-        copy.wait_recv()
-    for copy in tok_copies + cot_copies:
-        copy.wait_send()
+    away = cot_s.at[pl.ds(0, 3 * rows_loc)]
+    landed(away, arecv.at[2])
+    landed(away, asend.at[0])
+    landed(away, asend.at[1])
 
     def second_norm(i, carry):
         at = pl.ds(aligned(128 * i, 128), 128)
@@ -422,22 +407,20 @@
 
     given = []
 
-    def give_back(src, dst, base):
+    def give_back(src, dst, group):
         for k in (2, 3, 1):
             other = sp_xor(k)
-            copy = pltpu.make_async_remote_copy(
+            pltpu.make_async_remote_copy(
                 src_ref=src.at[other],
                 dst_ref=dst.at[sp],
-                send_sem=asend.at[base + k - 1],
-                recv_sem=arecv.at[base + k - 1],
+                send_sem=asend.at[group],
+                recv_sem=arecv.at[group + 1],
                 device_id=(dp, other),
                 device_id_type=MESH_ID,
-            )
-            copy.start()
-            given.append(copy)
-        own = pltpu.make_async_copy(src.at[sp], dst.at[sp], lsem.at[len(UNITS) + base // 3 - 2, 0])
+            ).start()
+        own = pltpu.make_async_copy(src.at[sp], dst.at[sp], lsem.at[group - 1])
         own.start()
-        given.append(own)
+        given.append((group, dst, own))
 
     def grad_down(j, first, size):
         r = nn(df_t[pl.ds(first, size), :], act_s[j]).astype(BF)
@@ -545,11 +528,13 @@
         else:
             vec_copies[i - 1].wait_recv()
             vl[i] = vl[i - 1] + vl[i]
+        if i == 5:
+            load(vl.at[5], gv_out, 11)
         if i < 5:
             copy = pltpu.make_async_remote_copy(
                 src_ref=vl.at[i],
                 dst_ref=vl.at[i + 1],
-                send_sem=vsend.at[i],
+                send_sem=vsend.at[0],
                 recv_sem=vrecv.at[i],
                 device_id=peer(VEC_PATH[i]),
                 device_id_type=MESH_ID,
@@ -611,18 +596,22 @@
         elif name == "X":
             transpose_tokens()
         elif name == "M":
-            give_back(tokp, mix_out, 6)
+            give_back(tokp, mix_out, 2)
         elif name == "K":
-            give_back(cotp, dtok_out, 9)
+            give_back(cotp, dtok_out, 3)
         elif name == "V":
             vec_step(at)
-    gv_out[...] = vl[5].astype(F32)
+    landed(gv_out, wsem.at[11])
+    final = p_s.at[pl.ds(0, 2), pl.ds(0, width * 9 // 16)]
+    landed(final, ufin.at[0])
+    landed(final, lsem.at[0])
     for n in range(len(UNITS)):
         finish(n)
-    for copy in vec_copies:
-        copy.wait_send()
-    for copy in given:
-        copy.wait()
+    landed(vl.at[pl.ds(0, 5)], vsend.at[0])
+    for group, dst, own in given:
+        landed(tokp.at[pl.ds(0, 3)], asend.at[group])
+        landed(dst.at[pl.ds(0, 3)], arecv.at[group + 1])
+        own.wait()
 
 
 def finish_kernel(*refs):
@@ -634,11 +623,17 @@
     held = [next(it) for _ in range(7)]
     staged = [next(it) for _ in range(5)]
     isem, osem = next(it), next(it)
-    loads = [pltpu.make_async_copy(src, dst, isem.at[i]) for i, (src, dst) in enumerate(zip(sources, held))]
-    for copy in loads:
-        copy.start()
     mix, dtok, go, gp, gu, gd, gv = held
     s_mix, s_dtok, s_sq, s_up, s_down = staged
+    part = gu.shape[1] // 2
+    pieces = [(4, (slice(None), pl.ds(i * part, part))) for i in range(2)] + [(5, (j,)) for j in range(3)]
+    pieces += [(3, (w,)) for w in range(3)] + [(i, ()) for i in (2, 0, 1, 6)]
+    loads = []
+    for i, at in pieces:
+        src, dst = (sources[i].at[at], held[i].at[at]) if at else (sources[i], held[i])
+        copy = pltpu.make_async_copy(src, dst, isem.at[len(loads)])
+        copy.start()
+        loads.append(copy)
     width = mix.shape[2]
     rows = width // 8
     dp = lax.axis_index("dp")
@@ -649,30 +644,31 @@
         copy.start()
         stores.append(copy)
 
-    loads[4].wait()
+    for i in range(2):
+        loads[i].wait()
+        at = slice(part * i, part * i + part)
+        for j in range(3):
+            for r in range(8):
+                s_up[at, 384 * r + 128 * j : 384 * r + 128 * j + 128] = gu[j, at, 128 * r : 128 * r + 128].astype(F32)
+        store(s_up.at[pl.ds(part * i, part)], o_up.at[pl.ds(part * i, part)])
     for j in range(3):
-        for r in range(8):
-            s_up[:, 384 * r + 128 * j : 384 * r + 128 * j + 128] = gu[j, :, 128 * r : 128 * r + 128].astype(F32)
-    store(s_up, o_up)
-    loads[5].wait()
-    for j in range(3):
+        loads[2 + j].wait()
         s_down[128 * j : 128 * j + 128, :] = gd[j].astype(F32).T
-    store(s_down, o_down)
-    loads[3].wait()
-    loads[2].wait()
+        store(s_down.at[pl.ds(128 * j, 128)], o_down.at[pl.ds(128 * j, 128)])
     for w in range(4):
+        loads[5 + w].wait()
         s_sq[w] = (go[...] if w == 3 else gp[w]).astype(F32)
         store(s_sq.at[w], (o_wq, o_wk, o_wv, o_wo)[w])
-    loads[0].wait()
+    loads[9].wait()
     s_mix[...] = jnp.swapaxes(mix[...], 0, 1)
     store(s_mix, o_mix)
-    loads[1].wait()
+    loads[10].wait()
     s_dtok[...] = jnp.swapaxes(dtok[...], 0, 1)
     store(s_dtok, o_dtok)
-    loads[6].wait()
+    loads[11].wait()
     for j in range(3):
-        o_bup[pl.ds(128 * j, 128)] = gv[pl.ds(10 + j, 1), pl.ds(aligned(dp * 128), 128)].reshape(128)
-    turned = pltpu.roll(gv[pl.ds(0, 8), pl.ds(0, width)], lax.rem(width - rows * dp, width), axis=1)
+        o_bup[pl.ds(128 * j, 128)] = gv[pl.ds(10 + j, 1), pl.ds(aligned(dp * 128), 128)].astype(F32).reshape(128)
+    turned = pltpu.roll(gv[pl.ds(0, 8), pl.ds(0, width)].astype(F32), lax.rem(width - rows * dp, width), axis=1)
     for i, ref in enumerate((o_bq, o_bv, o_bo, o_ga, o_sa, o_bdown, o_gf, o_sf)):
         ref[...] = turned[i : i + 1, :rows].reshape(rows)
     for copy in stores:
@@ -712,7 +708,7 @@
             scratch.append(vm(land_shape(unit, path, 4, rows, width)))
     dma = pltpu.SemaphoreType.DMA
     count = len(UNITS)
-    scratch += [dma((40,)), dma((count + 2, 2)), dma((15,)), dma((15,)), dma((count, 8)), dma((count, 8)), dma((5,)), dma((5,))]
+    scratch += [dma((12,)), dma((3,)), dma((4,)), dma((5,)), dma((count,)), dma((count, 6)), dma((1,)), dma((1,)), dma((5,))]
     anywhere = pl.BlockSpec(memory_space=pl.ANY)
     vmem = pl.BlockSpec(memory_space=pltpu.VMEM)
     got = pl.pallas_call(
@@ -724,10 +720,10 @@
             jax.ShapeDtypeStruct((3, rows, width), BF),
             jax.ShapeDtypeStruct((3, rows, CHUNK), BF),
             jax.ShapeDtypeStruct((3, width, 128), BF),
-            jax.ShapeDtypeStruct((ROWS_VEC, CHUNK), F32),
+            jax.ShapeDtypeStruct((ROWS_VEC, CHUNK), BF),
         ),
         in_specs=[pl.BlockSpec(memory_space=pltpu.SMEM)] + [vmem] * 9 + [anywhere] * 8,
-        out_specs=(anywhere,) * 6 + (vmem,),
+        out_specs=(anywhere,) * 7,
         scratch_shapes=scratch,
         compiler_params=pltpu.CompilerParams(collective_id=0, has_side_effects=True, vmem_limit_bytes=63 * 2**20),
     )(*args)
@@ -748,7 +744,7 @@
         scratch_shapes=[vm(value.shape, value.dtype) for value in got]
         + [
             vm((rows_loc, 4, width)), vm((rows_loc, 4, width)), vm((4, rows, width), F32),
-            vm((rows, 3 * CHUNK), F32), vm((384, width), F32), dma((7,)), dma((8,)),
+            vm((rows, 3 * CHUNK), F32), vm((384, width), F32), dma((12,)), dma((11,)),
         ],
         compiler_params=pltpu.CompilerParams(vmem_limit_bytes=63 * 2**20),
     )(*got)

time: 113 us -> 109 us (0.965)
  Pallas kernels: 112 us -> 108 us
    pallas_call x1, Pallas kernels: 107 us -> 104 us  [fused(): pl.pallas_call(layer_kernel, out_shape=(jax.ShapeDtypeStruct(swapped, BF)...]
where the time goes in v1:
time: 109 us
  Pallas kernels  108 us (99%)
    pallas_call x1, Pallas kernels, fused(): pl.pallas_call(layer_kernel, out_shape=(jax.ShapeDtypeStruct(swapped, BF)...  104 us
    pallas_call x1, Pallas kernels, fused(): pl.pallas_call(finish_kernel, out_shape=(whole, whole, flat, small, flat,...  4.1 us

profile of v1, /device:TPU:0, one launch (start us, length us, event | category | flops | bytes accessed | tf_op | source)
XLA Modules:
  0.0 109.1 jit_solution(6147017892352446650)
XLA Ops:
  0.7 104.2 %shard_map.305 = (bf16[4,128,768]{2,1,0:T(8,128)(2,1)}, bf16[4,128,768]{2,1,0:T(8,128)(2,1)}, bf16[96,768]{1,0:T(8,128)(2,1)}, bf16[3,96,768]{2,1,0:T(8,128)(2,1...) custom-call(s32[4]{0:T(128)} %refs_0_.1, bf16[768]{0:T(1024)(128)(2,1)} %refs_1_.1, ...), custom_call_target="tpu_custom_call" | custom-call | tf_op jit(solution)/shard_map/pallas_call | solution.py:714
  104.8 4.1 %shard_map.306 = (bf16[128,4,768]{2,1,0:T(4,128)(2,1)}, bf16[128,4,768]{2,1,0:T(4,128)(2,1)}, f32[96,768]{1,0:T(8,128)}, f32[96]{0:T(128)}, f32[96,768]{1,0:T(8,...) custom-call(bf16[4,128,768]{2,1,0:T(8,128)(2,1)} %get-tuple-element., ...), custom_call_target="tpu_custom_call" | custom-call | tf_op jit(solution)/shard_map/pallas_call | solution.py:733

commit v2 on v1

--- a/solution.py
+++ b/solution.py
@@ -32,22 +32,23 @@
 
 
 UNITS = (
-    ("d", 0, 0, 256), ("d", 0, 256, 256), ("d", 0, 512, 256), ("d", 1, 0, 384), ("d", 1, 384, 384), ("d", 2, 0, 384),
-    ("d", 2, 384, 384), ("u", 0, 0, 1024), ("u", 1, 0, 1024), ("u", 2, 0, 1024), ("o",), ("p", 0, 3, 0),
-    ("p", 0, 1, 1), ("p", 1, 2, 1), ("p", 0, 1, 2), ("p", 1, 1, 2), ("p", 2, 1, 2),
+    ("d", 0, 0, 256), ("d", 0, 256, 256), ("d", 0, 512, 256), ("d", 1, 0, 256), ("d", 1, 256, 256),
+    ("d", 1, 512, 256), ("d", 2, 0, 256), ("d", 2, 256, 256), ("d", 2, 512, 256), ("u", 0, 0, 1024),
+    ("u", 1, 0, 1024), ("u", 2, 0, 1024), ("o",), ("p", 0, 3, 0), ("p", 0, 1, 1), ("p", 1, 2, 1), ("p", 0, 1, 2),
+    ("p", 1, 1, 2), ("p", 2, 1, 2),
 )
 PATH = (
-    "c102y", "c120Y", "c0y12", "c102y", "c0y12", "cy120", "c01y2", "cy120", "cy012", "c0y12", "c120Y", "c012y",
-    "c012y", "c0y12", "c012Y", "c0y12", "c0y12",
+    "c102Y", "c10y2", "c01y2", "c102y", "cy012", "cy120", "c01y2", "cy102", "c120Y", "c01y2", "c012y", "cy012",
+    "c102y", "cy012", "c120Y", "cy012", "c01y2", "c01y2", "c0y12",
 )
 ORDER = (
-    "M", 0, 1, 2, 3, 0, 1, 2, 4, 5, 6, "X", "I0", 3, 4, "I1", 5, 6, 0, 2, "H0", 1, 7, 4, 8, 5, 3, 7, 2, 9, "F", 6, 1,
-    8, 4, 0, "A", 9, 5, 2, 10, 3, 1, "B0", 6, 4, 10, 0, 11, 5, 2, "B2", 7, 3, 11, 4, 12, 9, 5, 13, "B4", 12, 13, 10,
-    8, "T", "K", 1, 6, 0, 2, 7, 3, 11, 4, 14, 15, 16, "V0", 12, 14, 15, 16, "V1", 9, 5, 10, 13, 6, 11, 12, 8, 7, 9,
-    14, 0, 11, 3, 15, 12, 8, 13, 6, 16, 9, "V2", 11, 14, 15, 12, 10, 13, 16, 7, 8, "V3", 9, 14, 15, 11, 12, 16, 13,
-    10, 7, "V4", 15, 8, 16, 14, 13, "V5", 15, 16,
+    "M", 0, 1, 2, "X", 0, "I0", 1, 2, 3, 4, 5, 6, 7, 8, "I1", 3, 0, 4, 5, 6, 2, 7, "H0", 8, 1, 0, 9, 3, 4, 10, 2, 6,
+    1, 9, 5, 11, "F", 8, 3, 10, 0, 4, 7, 6, "A", 11, 2, 1, 5, 12, 0, "B0", 6, 4, 8, 12, 7, 3, 2, 13, 1, "B2", 9, 5, 6,
+    13, 4, 14, 11, 3, 2, 15, "B4", 1, 6, 14, 15, 12, 10, "T", "K", 8, 7, 5, 9, 16, 13, 4, 3, 17, 18, "V0", 14, 16, 17,
+    11, 18, "V1", 15, 10, 12, 7, 14, 13, 11, 16, 10, 17, 8, 5, 13, 18, 12, "V2", 9, 16, 7, 17, 11, 10, 15, 14, 18,
+    "V3", 13, 12, 16, 17, 15, 9, 18, 11, 10, "V4", 14, 16, 17, 13, 12, 15, 18, 9, "V5", 16, 17, 15, 18,
 )
-VEC_PATH = "c012y"
+VEC_PATH = "c120y"
 ROWS_VEC = 16
 CHUNK = 1024
 ATTEND = 6

time: 109 us -> 109 us (level)
  no operation moved by 1% of the time
where the time goes in v2:
time: 109 us; the launch traced here: 108 us
  Pallas kernels  107 us (98%)
    pallas_call x1, Pallas kernels, fused(): pl.pallas_call(layer_kernel, out_shape=(jax.ShapeDtypeStruct(swapped, BF)...  103 us
    pallas_call x1, Pallas kernels, fused(): pl.pallas_call(finish_kernel, out_shape=(whole, whole, flat, small, flat,...  4.1 us

profile of v2, /device:TPU:0, one launch (start us, length us, event | category | flops | bytes accessed | tf_op | source)
XLA Modules:
  0.0 108.3 jit_solution(1380497361684439457)
XLA Ops:
  0.7 103.4 %shard_map.305 = (bf16[4,128,768]{2,1,0:T(8,128)(2,1)}, bf16[4,128,768]{2,1,0:T(8,128)(2,1)}, bf16[96,768]{1,0:T(8,128)(2,1)}, bf16[3,96,768]{2,1,0:T(8,128)(2,1...) custom-call(s32[4]{0:T(128)} %refs_0_.1, bf16[768]{0:T(1024)(128)(2,1)} %refs_1_.1, ...), custom_call_target="tpu_custom_call" | custom-call | tf_op jit(solution)/shard_map/pallas_call | solution.py:715
  104.1 4.1 %shard_map.306 = (bf16[128,4,768]{2,1,0:T(4,128)(2,1)}, bf16[128,4,768]{2,1,0:T(4,128)(2,1)}, f32[96,768]{1,0:T(8,128)}, f32[96]{0:T(128)}, f32[96,768]{1,0:T(8,...) custom-call(bf16[4,128,768]{2,1,0:T(8,128)(2,1)} %get-tuple-element., ...), custom_call_target="tpu_custom_call" | custom-call | tf_op jit(solution)/shard_map/pallas_call | solution.py:734

commit v3 on v2

--- a/solution.py
+++ b/solution.py
@@ -97,6 +97,7 @@
     vs, vl = next(it), next(it)
     lands = [[next(it) for _ in path] for path in PATH]
     tails = [next(it) if "y" in path else None for path in PATH]
+    len_s = next(it)
     (wsem, lsem, asend, arecv, usend, urecv, ufin, vsend, vrecv) = (next(it) for _ in range(9))
 
     rows_loc, width = tok_ref.shape[0], tok_ref.shape[2]
@@ -138,6 +139,7 @@
 
     quick = rows_loc // 2
     tok_loads = [load(tok_ref.at[pl.ds(i * quick, quick)], raw_s.at[pl.ds(i * quick, quick)], i) for i in range(2)]
+    len_load = load(len_ref, len_s, 12)
     attn_loads = [load(ref, wa.at[i], 2 + i) for i, ref in enumerate((wq_ref, wk_ref, wv_ref, wo_ref))]
 
     def exchange(src, dst, group, first=0, size=rows_loc):
@@ -274,7 +276,8 @@
         vs[0, pl.ds(row, 1), pl.ds(0, value.shape[1])] = value
 
     vs[0] = jnp.zeros(vs.shape[1:], F32)
-    length = len_ref[sp]
+    len_load.wait()
+    length = len_s[sp]
     dead = lax.broadcasted_iota(jnp.int32, (total, 128), 0) >= length
     km_s[...] = jnp.where(dead, -1e30, 0.0).astype(BF)
     ones = jnp.ones((16, total), BF)
@@ -709,7 +712,8 @@
             scratch.append(vm(land_shape(unit, path, 4, rows, width)))
     dma = pltpu.SemaphoreType.DMA
     count = len(UNITS)
-    scratch += [dma((12,)), dma((3,)), dma((4,)), dma((5,)), dma((count,)), dma((count, 6)), dma((1,)), dma((1,)), dma((5,))]
+    scratch.append(pltpu.SMEM((4,), jnp.int32))
+    scratch += [dma((13,)), dma((3,)), dma((4,)), dma((5,)), dma((count,)), dma((count, 6)), dma((1,)), dma((1,)), dma((5,))]
     anywhere = pl.BlockSpec(memory_space=pl.ANY)
     vmem = pl.BlockSpec(memory_space=pltpu.VMEM)
     got = pl.pallas_call(
@@ -723,7 +727,7 @@
             jax.ShapeDtypeStruct((3, width, 128), BF),
             jax.ShapeDtypeStruct((ROWS_VEC, CHUNK), BF),
         ),
-        in_specs=[pl.BlockSpec(memory_space=pltpu.SMEM)] + [vmem] * 9 + [anywhere] * 8,
+        in_specs=[anywhere] + [vmem] * 9 + [anywhere] * 8,
         out_specs=(anywhere,) * 7,
         scratch_shapes=scratch,
         compiler_params=pltpu.CompilerParams(collective_id=0, has_side_effects=True, vmem_limit_bytes=63 * 2**20),

time: 109 us -> 109 us (level)
  no operation moved by 1% of the time
where the time goes in v3:
time: 109 us
  Pallas kernels  108 us (99%)
    pallas_call x1, Pallas kernels, fused(): pl.pallas_call(layer_kernel, out_shape=(jax.ShapeDtypeStruct(swapped, BF)...  104 us
    pallas_call x1, Pallas kernels, fused(): pl.pallas_call(finish_kernel, out_shape=(whole, whole, flat, small, flat,...  4.1 us

profile of v3, /device:TPU:0, one launch (start us, length us, event | category | flops | bytes accessed | tf_op | source)
XLA Modules:
  0.0 108.6 jit_solution(11970717040039764946)
XLA Ops:
  0.7 103.6 %shard_map.305 = (bf16[4,128,768]{2,1,0:T(8,128)(2,1)}, bf16[4,128,768]{2,1,0:T(8,128)(2,1)}, bf16[96,768]{1,0:T(8,128)(2,1)}, bf16[3,96,768]{2,1,0:T(8,128)(2,1...) custom-call(s32[4]{0:T(128)} %refs_0_.1, bf16[768]{0:T(1024)(128)(2,1)} %refs_1_.1, ...), custom_call_target="tpu_custom_call" | custom-call | tf_op jit(solution)/shard_map/pallas_call | solution.py:719
  104.3 4.1 %shard_map.306 = (bf16[128,4,768]{2,1,0:T(4,128)(2,1)}, bf16[128,4,768]{2,1,0:T(4,128)(2,1)}, f32[96,768]{1,0:T(8,128)}, f32[96]{0:T(128)}, f32[96,768]{1,0:T(8,...) custom-call(bf16[4,128,768]{2,1,0:T(8,128)(2,1)} %get-tuple-element., ...), custom_call_target="tpu_custom_call" | custom-call | tf_op jit(solution)/shard_map/pallas_call | solution.py:738
